TPU v7x, 512 devices: a whole 4x8x8 slice. The times are simulated.
512 devices in a mesh: dp: 16 (over z_hi, x, core), tensor: 32 (over y, z_lo).
Axes of the slice: x: 4, y: 8, z: 8 (z_hi: 2, z_lo: 4; z = z_hi * 4 + z_lo), core: 2. Of those that a mesh axis runs over, the one named last changes fastest.
Arguments:
- hidden_rows: bfloat16 [4096, 28672], P('dp', 'tensor'), may hold values from -6 to 6
- out_grads: bfloat16 [4096, 8192], P('dp', 'tensor'), may hold values from -6 to 6
- proj_in: bfloat16 [28672, 64], P('tensor'), may hold values from -1 to 1
- proj_out: bfloat16 [8192, 64], P('tensor'), may hold values from -1 to 1
- queries: float32 [4096, 256], P('tensor', 'dp'), may hold values from -6 to 6
Outputs:
- precond: float32 [4096, 256], P('tensor', 'dp')
- scores: float32 [256, 16], P('tensor', 'dp')
All inputs are finite; a program needn't handle non-finite values.
Results may differ from a plain program's by a relative error of at most 0.0073.
Values may be sent and summed in bfloat16 or wider, within the bound.
A program may use at most 64 MiB of HBM per device.

v0:
```python
import jax
import jax.numpy as jnp
from jax import lax
from jax.sharding import PartitionSpec as P

SEQ_LEN = 256
ITERS = 8


damping = 0.5
highest = lax.Precision.HIGHEST


def kron_rows(hid_rows, grad_rows):
    outer_prod = (
        hid_rows.astype(jnp.float32)[:, :, None] * grad_rows.astype(jnp.float32)[:, None, :]
    )
    return outer_prod.reshape(hid_rows.shape[0], hid_rows.shape[1] * grad_rows.shape[1]).astype(
        jnp.bfloat16
    )


def fold_sequences(running, hid_rows, grad_rows, own_offset, own_columns):
    seq_count = hid_rows.shape[0] // SEQ_LEN

    def absorb(carried, pieces):
        kron_full = kron_rows(pieces[0], pieces[1])
        kron_own = lax.dynamic_slice_in_dim(kron_full, own_offset, own_columns, 1)
        carried = carried + lax.dot_general(
            kron_own, kron_full, (((0,), (0,)), ((), ())), preferred_element_type=jnp.float32
        )
        return (carried, jnp.sum(kron_own.astype(jnp.float32), axis=0) / SEQ_LEN)

    stacked = (
        hid_rows.reshape(seq_count, SEQ_LEN, hid_rows.shape[1]),
        grad_rows.reshape(seq_count, SEQ_LEN, grad_rows.shape[1]),
    )
    return lax.scan(absorb, running, stacked)


def shards(hidden_rows, out_grads, proj_in, proj_out, queries):
    hid_part = jnp.dot(hidden_rows, proj_in, preferred_element_type=jnp.float32)
    grad_part = jnp.dot(out_grads, proj_out, preferred_element_type=jnp.float32)
    hid_sum, grad_sum = lax.psum((hid_part, grad_part), "tensor")
    hid_proj = hid_sum.astype(jnp.bfloat16)
    grad_proj = grad_sum.astype(jnp.bfloat16)
    proj_rank = hid_proj.shape[1]
    own_rank = proj_rank // lax.axis_size("tensor")
    own_columns = own_rank * proj_rank
    own_offset = lax.axis_index("tensor") * own_columns
    zero_rows = jnp.zeros((own_columns, proj_rank * proj_rank), jnp.float32)
    local_sum, seq_feats = fold_sequences(zero_rows, hid_proj, grad_proj, own_offset, own_columns)
    fisher_sum = lax.psum(local_sum, "dp")
    fisher_rows = fisher_sum / (hidden_rows.shape[0] * lax.axis_size("dp"))

    def squares(vectors):
        return lax.psum(jnp.sum(vectors * vectors, axis=0), "tensor")

    solution = jnp.zeros_like(queries)
    residual = queries
    direction = queries
    norm_now = squares(residual)
    for iteration in range(ITERS):
        product = jnp.dot(
            fisher_rows, lax.all_gather(direction, "tensor", axis=0, tiled=True), precision=highest
        )
        applied = product + damping * direction
        step_size = norm_now / lax.psum(jnp.sum(direction * applied, axis=0), "tensor")
        solution = solution + step_size * direction
        residual = residual - step_size * applied
        norm_next = squares(residual)
        direction = residual + norm_next / norm_now * direction
        norm_now = norm_next
    partial_scores = jnp.dot(
        lax.all_gather(solution, "dp", axis=1, tiled=True).T, seq_feats.T, precision=highest
    )
    scores = lax.psum_scatter(partial_scores, "tensor", scatter_dimension=0, tiled=True)
    return (solution, scores)


def solution(mesh):
    return jax.shard_map(
        shards,
        mesh=mesh,
        in_specs=(
            P("dp", "tensor"),
            P("dp", "tensor"),
            P("tensor", None),
            P("tensor", None),
            P("tensor", "dp"),
        ),
        out_specs=(P("tensor", "dp"), P("tensor", "dp")),
        check_vma=False,
    )
```

profile of v0, /device:TPU:1, one launch (start us, length us, event | category | flops | bytes accessed | tf_op | source)
XLA Modules:
  0.0 2133.2 jit_solution(14626314604174430224)
XLA Ops:
  10.4 129.0 %all-reduce.7 = (bf16[256,64]{0,1:T(8,128)(2,1)S(1)}, bf16[256,64]{0,1:T(8,128)(2,1)S(1)}) all-reduce(f32[256,64]{0,1:T(8,128)S(1)} %fusion.70, f32[256,64]{0,1:T(8,128)S(1)} %fusion.69), channel_id=1, replica_groups=mesh['dp'=16,'tensor'=32] {'tensor'}, use_global_device_ids=true, to_apply=%region_3.0 | all-reduce | flops 32768 | bytes 196608 | tf_op jit(solution)/shard_map/psum | solution.py:44
  140.2 2.1 fusion.54
  144.4 61.4 %all_gather.27 = f32[4096,16]{0,1:T(8,128)S(1)} all-gather(f32[128,16]{0,1:T(8,128)S(1)} %copy-done.2), channel_id=1, replica_groups=mesh['dp'=16,'tensor'=32] {'tensor'}, dimensions={0}, use_global_device_ids=true | all-gather | bytes 270336 | tf_op jit(solution)/shard_map/all_gather | solution.py:65
  205.7 154.3 %all-reduce.6.cloned.1.call-done = f32[128,4096]{1,0:T(8,128)} async-done(((f32[128,4096]{1,0:T(8,128)}), f32[128,4096]{1,0:T(8,128)}) %all-reduce.6.cloned.1.call-update) | async-done | bytes 2097168 | tf_op jit(solution)/shard_map/psum | solution.py:53
  360.1 3.6 multiply_reduce_fusion.13
  363.7 63.8 %all-reduce.1 = (f32[16]{0:T(128)S(1)}, f32[16]{0:T(128)S(1)}) all-reduce(f32[16]{0:T(128)S(1)} %get-tuple-element.15, f32[16]{0:T(128)S(1)} %get-tuple-element.14), channel_id=1, replica_groups=mesh['dp'=16,'tensor'=32] {'tensor'}, use_global_device_ids=true, to_apply=%region_1.0 | all-reduce | flops 32 | bytes 256 | tf_op jit(solution)/shard_map/psum | solution.py:57
  427.7 60.5 %psum.138 = f32[16]{0:T(128)S(1)} all-reduce(f32[16]{0:T(128)S(1)} %multiply_reduce_fusion.12), channel_id=1, replica_groups=mesh['dp'=16,'tensor'=32] {'tensor'}, use_global_device_ids=true, to_apply=%region_8.9 | all-reduce | flops 16 | bytes 128 | tf_op jit(solution)/shard_map/psum | solution.py:57
  488.3 62.1 %all_gather.28 = f32[4096,16]{0,1:T(8,128)S(1)} all-gather(f32[128,16]{0,1:T(8,128)S(1)} %multiply_add_fusion.7), channel_id=1, replica_groups=mesh['dp'=16,'tensor'=32] {'tensor'}, dimensions={0}, use_global_device_ids=true | all-gather | bytes 270336 | tf_op jit(solution)/shard_map/all_gather | solution.py:65
  550.4 1.9 multiply_reduce_fusion.11
  552.2 60.7 %psum.139 = f32[16]{0:T(128)S(1)} all-reduce(f32[16]{0:T(128)S(1)} %get-tuple-element.37), channel_id=1, replica_groups=mesh['dp'=16,'tensor'=32] {'tensor'}, use_global_device_ids=true, to_apply=%region_10.11 | all-reduce | flops 16 | bytes 128 | tf_op jit(solution)/shard_map/psum | solution.py:68
  613.1 62.2 %psum.140 = f32[16]{0:T(128)S(1)} all-reduce(f32[16]{0:T(128)S(1)} %get-tuple-element.34), channel_id=1, replica_groups=mesh['dp'=16,'tensor'=32] {'tensor'}, use_global_device_ids=true, to_apply=%region_12.13 | all-reduce | flops 16 | bytes 128 | tf_op jit(solution)/shard_map/psum | solution.py:57
  675.4 60.7 %all_gather.29 = f32[4096,16]{0,1:T(8,128)S(1)} all-gather(f32[128,16]{0,1:T(8,128)S(1)} %multiply_add_fusion.6), channel_id=1, replica_groups=mesh['dp'=16,'tensor'=32] {'tensor'}, dimensions={0}, use_global_device_ids=true | all-gather | bytes 270336 | tf_op jit(solution)/shard_map/all_gather | solution.py:65
  736.1 1.9 multiply_reduce_fusion.9
  737.9 62.6 %psum.141 = f32[16]{0:T(128)S(1)} all-reduce(f32[16]{0:T(128)S(1)} %get-tuple-element.39), channel_id=1, replica_groups=mesh['dp'=16,'tensor'=32] {'tensor'}, use_global_device_ids=true, to_apply=%region_14.15 | all-reduce | flops 16 | bytes 128 | tf_op jit(solution)/shard_map/psum | solution.py:68
  800.7 60.6 %psum.142 = f32[16]{0:T(128)S(1)} all-reduce(f32[16]{0:T(128)S(1)} %get-tuple-element.32), channel_id=1, replica_groups=mesh['dp'=16,'tensor'=32] {'tensor'}, use_global_device_ids=true, to_apply=%region_16.17 | all-reduce | flops 16 | bytes 128 | tf_op jit(solution)/shard_map/psum | solution.py:57
  861.4 62.0 %all_gather.30 = f32[4096,16]{0,1:T(8,128)S(1)} all-gather(f32[128,16]{0,1:T(8,128)S(1)} %multiply_add_fusion.5), channel_id=1, replica_groups=mesh['dp'=16,'tensor'=32] {'tensor'}, dimensions={0}, use_global_device_ids=true | all-gather | bytes 270336 | tf_op jit(solution)/shard_map/all_gather | solution.py:65
  923.4 1.9 multiply_reduce_fusion.7
  925.3 60.5 %psum.143 = f32[16]{0:T(128)S(1)} all-reduce(f32[16]{0:T(128)S(1)} %get-tuple-element.41), channel_id=1, replica_groups=mesh['dp'=16,'tensor'=32] {'tensor'}, use_global_device_ids=true, to_apply=%region_18.19 | all-reduce | flops 16 | bytes 128 | tf_op jit(solution)/shard_map/psum | solution.py:68
  986.0 61.9 %psum.144 = f32[16]{0:T(128)S(1)} all-reduce(f32[16]{0:T(128)S(1)} %get-tuple-element.30), channel_id=1, replica_groups=mesh['dp'=16,'tensor'=32] {'tensor'}, use_global_device_ids=true, to_apply=%region_20.21 | all-reduce | flops 16 | bytes 128 | tf_op jit(solution)/shard_map/psum | solution.py:57
  1047.9 60.6 %all_gather.31 = f32[4096,16]{0,1:T(8,128)S(1)} all-gather(f32[128,16]{0,1:T(8,128)S(1)} %multiply_add_fusion.4), channel_id=1, replica_groups=mesh['dp'=16,'tensor'=32] {'tensor'}, dimensions={0}, use_global_device_ids=true | all-gather | bytes 270336 | tf_op jit(solution)/shard_map/all_gather | solution.py:65
  1110.4 61.8 %psum.145 = f32[16]{0:T(128)S(1)} all-reduce(f32[16]{0:T(128)S(1)} %get-tuple-element.43), channel_id=1, replica_groups=mesh['dp'=16,'tensor'=32] {'tensor'}, use_global_device_ids=true, to_apply=%region_22.23 | all-reduce | flops 16 | bytes 128 | tf_op jit(solution)/shard_map/psum | solution.py:68
  1172.4 60.8 %psum.146 = f32[16]{0:T(128)S(1)} all-reduce(f32[16]{0:T(128)S(1)} %get-tuple-element.28), channel_id=1, replica_groups=mesh['dp'=16,'tensor'=32] {'tensor'}, use_global_device_ids=true, to_apply=%region_24.25 | all-reduce | flops 16 | bytes 128 | tf_op jit(solution)/shard_map/psum | solution.py:57
  1233.2 61.5 %all_gather.32 = f32[4096,16]{0,1:T(8,128)S(1)} all-gather(f32[128,16]{0,1:T(8,128)S(1)} %multiply_add_fusion.3), channel_id=1, replica_groups=mesh['dp'=16,'tensor'=32] {'tensor'}, dimensions={0}, use_global_device_ids=true | all-gather | bytes 270336 | tf_op jit(solution)/shard_map/all_gather | solution.py:65
  1296.6 60.9 %psum.147 = f32[16]{0:T(128)S(1)} all-reduce(f32[16]{0:T(128)S(1)} %get-tuple-element.45), channel_id=1, replica_groups=mesh['dp'=16,'tensor'=32] {'tensor'}, use_global_device_ids=true, to_apply=%region_26.27 | all-reduce | flops 16 | bytes 128 | tf_op jit(solution)/shard_map/psum | solution.py:68
  1357.7 61.5 %psum.148 = f32[16]{0:T(128)S(1)} all-reduce(f32[16]{0:T(128)S(1)} %get-tuple-element.26), channel_id=1, replica_groups=mesh['dp'=16,'tensor'=32] {'tensor'}, use_global_device_ids=true, to_apply=%region_28.29 | all-reduce | flops 16 | bytes 128 | tf_op jit(solution)/shard_map/psum | solution.py:57
  1419.3 61.0 %all_gather.33 = f32[4096,16]{0,1:T(8,128)S(1)} all-gather(f32[128,16]{0,1:T(8,128)S(1)} %multiply_add_fusion.2), channel_id=1, replica_groups=mesh['dp'=16,'tensor'=32] {'tensor'}, dimensions={0}, use_global_device_ids=true | all-gather | bytes 270336 | tf_op jit(solution)/shard_map/all_gather | solution.py:65
  1482.2 61.6 %psum.149 = f32[16]{0:T(128)S(1)} all-reduce(f32[16]{0:T(128)S(1)} %get-tuple-element.47), channel_id=1, replica_groups=mesh['dp'=16,'tensor'=32] {'tensor'}, use_global_device_ids=true, to_apply=%region_30.31 | all-reduce | flops 16 | bytes 128 | tf_op jit(solution)/shard_map/psum | solution.py:68
  1544.0 61.1 %psum.150 = f32[16]{0:T(128)S(1)} all-reduce(f32[16]{0:T(128)S(1)} %multiply_reduce_fusion), channel_id=1, replica_groups=mesh['dp'=16,'tensor'=32] {'tensor'}, use_global_device_ids=true, to_apply=%region_32.33 | all-reduce | flops 16 | bytes 128 | tf_op jit(solution)/shard_map/psum | solution.py:57
  1605.2 61.4 %all_gather.34 = f32[4096,16]{0,1:T(8,128)S(1)} all-gather(f32[128,16]{0,1:T(8,128)S(1)} %multiply_add_fusion.1), channel_id=1, replica_groups=mesh['dp'=16,'tensor'=32] {'tensor'}, dimensions={0}, use_global_device_ids=true | all-gather | bytes 270336 | tf_op jit(solution)/shard_map/all_gather | solution.py:65
  1668.4 61.1 %psum.151 = f32[16]{0:T(128)S(1)} all-reduce(f32[16]{0:T(128)S(1)} %fusion.43), channel_id=1, replica_groups=mesh['dp'=16,'tensor'=32] {'tensor'}, use_global_device_ids=true, to_apply=%region_34.35 | all-reduce | flops 16 | bytes 128 | tf_op jit(solution)/shard_map/psum | solution.py:68
  1729.7 333.8 %all_gather.35 = f32[128,256]{0,1:T(8,128)S(1)} all-gather(f32[128,16]{0,1:T(8,128)S(1)} %multiply_add_fusion), channel_id=1, replica_groups=mesh['dp'=16,'tensor'=32] {'dp'}, dimensions={1}, use_global_device_ids=true | all-gather | bytes 139264 | tf_op jit(solution)/shard_map/all_gather | solution.py:75
  2063.7 62.1 %all-reduce = f32[256,1]{0,1:T(1,128)S(1)} all-reduce(f32[256,1]{0,1:T(1,128)S(1)} %convolution_bitcast_fusion), channel_id=2, replica_groups=mesh['dp'=16,'tensor'=32] {'tensor'}, use_global_device_ids=true, to_apply=%region_36.37.clone | all-reduce | flops 256 | bytes 2048
  (53 shorter events, 15.6 us)
Async XLA Ops:
  7.2 1.0 copy-start
  7.2 352.9 %all-reduce.6.cloned.1.call-start = ((), (), s32[]{:S(2)}) async-start(), calls=%async_computation | async-start | bytes 4194304 | tf_op jit(solution)/shard_map/psum | solution.py:53
  142.3 2.1 copy-start.2
  360.1 190.3 %copy-start.1 = (f32[128,4096]{1,0:T(8,128)S(1)}, f32[128,4096]{1,0:T(8,128)}, u32[]{:S(2)}) copy-start(f32[128,4096]{1,0:T(8,128)} %all-reduce.6.cloned.1.call-done) | copy-start | bytes 6291460
  1729.7 396.7 %copy-start.3 = (f32[128,16]{0,1:T(8,128)}, f32[128,16]{0,1:T(8,128)S(1)}, u32[]{:S(2)}) copy-start(f32[128,16]{0,1:T(8,128)S(1)} %multiply_add_fusion) | copy-start | bytes 24580
Sparse Core Ops, SparseCore 0:
  142.4 217.5 all-reduce.5
where the time goes:
time: 2150 us; the launch traced here: 2130 us
  blocking collectives  1940 us (90%)
  waiting for transfers between devices  154 us (7%)
    psum x8, blocking collectives, squares(): return lax.psum(jnp.sum(vectors * vectors, axis=0), 'tensor')  492 us
    all_gather x8, blocking collectives, shards(): lax.all_gather(direction, 'tensor', axis=0, tiled=True)  491 us
    psum x7, blocking collectives, shards(): lax.psum(jnp.sum(direction * applied, axis=0), 'tensor')  429 us
    all_gather x1, blocking collectives, shards(): lax.all_gather(solution, 'dp', axis=1, tiled=True)  334 us
    psum x1, waiting for transfers between devices, shards(): fisher_sum = lax.psum(local_sum, 'dp')  154 us
    psum x1, blocking collectives, shards(): hid_sum, grad_sum = lax.psum((hid_part, grad_part), 'tensor')  129 us
    unnamed x1, blocking collectives  62.1 us
  transfers between devices with their start and end apart: 1, of which 1 were waited for; matrix products, arithmetic and copies ran while one was open for 0% of the time, Pallas kernels for 0%

commit v1 on v0

v1 whole, which is shorter than its diff:
```python
import functools

import jax
import jax.numpy as jnp
from jax import lax
from jax.experimental import pallas as pl
from jax.experimental.pallas import tpu as pltpu
from jax.sharding import PartitionSpec as P

SEQ_LEN = 256
ITERS = 8
EXACT = 3
DAMPING = 0.5
F32 = jnp.float32
BF16 = jnp.bfloat16
MESH = pl.DeviceIdType.MESH

XS, CORES, YS, ZLO, ZHI = 4, 2, 8, 4, 2
GROUP = YS * ZLO
DPS = ZHI * XS * CORES
QUERIES = 16
SHARE = SEQ_LEN // YS
HALF = YS // 2
RANK = 64
LANES = 2 * RANK

NN = (((1,), (0,)), ((), ()))
NT = (((1,), (1,)), ((), ()))


def dot(left, right, dims=NN):
    return lax.dot_general(left, right, dims, preferred_element_type=F32)


def total(values):
    return jnp.sum(jnp.sum(values, axis=0, keepdims=True), axis=1, keepdims=True)


def kernel(
    hid_hbm, grad_hbm, pin_hbm, pout_hbm, query_hbm,
    sol_ref, score_ref,
    hid_v, grad_v, pin_v, pout_v, query_v,
    part, arrived, zparts, feats,
    query_out, query_mid, query_in, sol_out, sol_in, score_out, score_in,
    twice, hid_t,
    load_sem, ready_sem, rs_send, rs_recv, z_send, z_recv, q_send, q_recv, p_send, p_recv,
    y_send, y_recv, x_send, x_recv, c_send, c_recv, o_send, o_recv, s_send, s_recv,
):
    dp = lax.axis_index("dp")
    me = lax.axis_index("tensor")
    z_hi = dp // (XS * CORES)
    xc = lax.rem(dp, XS * CORES)
    x = xc // CORES
    core = lax.rem(dp, CORES)
    y = me // ZLO
    z_lo = lax.rem(me, ZLO)

    def pair_at(z_lo_of):
        return lax.rem(lax.rem((z_lo_of + 1) // 2 + 1, 2) + core, 2), lax.rem(z_lo_of, 2)

    score_half, odd = pair_at(z_lo)
    score_row = lax.rem(y, HALF) * 2 + odd
    query = score_half * 8 + score_row

    def at(dp_to, tensor_to):
        return {"dp": dp_to, "tensor": tensor_to}

    def send(src, dst, send_sem, recv_sem, device):
        pltpu.make_async_remote_copy(
            src_ref=src, dst_ref=dst, send_sem=send_sem, recv_sem=recv_sem,
            device_id=device, device_id_type=MESH,
        ).start()

    def wait(sem, like):
        pltpu.make_async_copy(like, like, sem).wait()

    y_peers = [lax.rem(y + k, YS) for k in (4, 3, 5, 2, 6, 1, 7)]
    z_peers = [lax.rem(z_lo + k, ZLO) for k in (2, 1, 3)]
    other_dp = (1 - z_hi) * (XS * CORES) + xc
    other = at(other_dp, y * ZLO + (ZLO - 1 - z_lo))
    right = at(z_hi * (XS * CORES) + lax.rem(x + 1, XS) * CORES + core, me)
    left = at(z_hi * (XS * CORES) + lax.rem(x + XS - 1, XS) * CORES + core, me)
    far = at(z_hi * (XS * CORES) + lax.rem(x + 2, XS) * CORES + core, me)
    twin = at(dp + 1 - 2 * core, me)

    barrier = pltpu.get_barrier_semaphore()
    greeted = [at(dp, to * ZLO + z_lo) for to in y_peers] + [at(dp, y * ZLO + to) for to in z_peers]
    greeted += [other, right, left, far, twin]
    for device in greeted:
        pl.semaphore_signal(barrier, inc=1, device_id=device, device_id_type=MESH)

    loads = [
        pltpu.make_async_copy(src, dst, load_sem.at[i])
        for i, (src, dst) in enumerate(
            ((hid_hbm, hid_v), (pin_hbm, pin_v), (grad_hbm, grad_v), (pout_hbm, pout_v), (query_hbm, query_v))
        )
    ]
    for load in loads:
        load.start()

    loads[0].wait()
    loads[1].wait()
    hid_part = dot(hid_v[...], pin_v[...], NT)
    loads[2].wait()
    loads[3].wait()
    grad_part = dot(grad_v[...], pout_v[...], NT)
    part[...] = jnp.concatenate([hid_part, grad_part], axis=1).reshape(YS, SHARE, LANES)

    pl.semaphore_wait(barrier, len(greeted))
    for k, to in enumerate(y_peers):
        send(part.at[to], arrived.at[k], rs_send, rs_recv, at(dp, to * ZLO + z_lo))

    loads[4].wait()
    query_rows = query_v[...]
    for i in range(QUERIES):
        query_out[i // 8, i % 8 // 2, i % 2] = query_rows[i : i + 1, :]
    for i in range(2):
        for j in range(2):
            query_mid[i, j, y] = query_out[i, lax.rem(y, HALF), j]
    for to in y_peers:
        send(
            query_out.at[:, lax.rem(to, HALF)], query_mid.at[:, :, y], q_send, q_recv,
            at(dp, to * ZLO + z_lo),
        )

    wait(rs_recv, arrived)
    pl.semaphore_signal(ready_sem, inc=1, device_id=other, device_id_type=MESH)
    zparts[z_lo] = part[y] + jnp.sum(arrived[...], axis=0)
    for to in z_peers:
        send(zparts.at[z_lo], zparts.at[z_lo], z_send, z_recv, at(dp, y * ZLO + to))

    wait(q_recv, query_mid.at[:, :, pl.ds(0, YS - 1)])
    for to in z_peers:
        send(query_mid.at[pair_at(to)], query_in.at[z_lo], p_send, p_recv, at(dp, y * ZLO + to))
    query_in[z_lo] = query_mid[score_half, odd]

    wait(z_recv, zparts.at[pl.ds(0, ZLO - 1)])
    mine = (xc * ZHI + z_hi) * YS + y
    feats[mine] = jnp.sum(zparts[...], axis=0).astype(BF16)
    pl.semaphore_wait(ready_sem, 1)

    spread = [(k, True) for k in (4, 3, 5)] + [(k, False) for k in (4, 3, 5)]
    spread += [(k, True) for k in (2, 6, 1, 7)] + [(k, False) for k in (2, 6, 1, 7, 0)]
    for k, same in spread:
        to = lax.rem(y + k, YS)
        if same:
            send(feats.at[mine], feats.at[mine], y_send, y_recv.at[0], at(dp, to * ZLO + z_lo))
        else:
            send(
                feats.at[mine], feats.at[mine], y_send, y_recv.at[1],
                at(other_dp, to * ZLO + (ZLO - 1 - z_lo)),
            )

    lane = lax.broadcasted_iota(jnp.int32, (RANK, LANES), 1)
    row = lax.broadcasted_iota(jnp.int32, (RANK, LANES), 0)
    low = lane < RANK
    pair = lax.rem(row, YS) * ZLO + lax.rem(row, GROUP) // YS
    select = jnp.where(lane == 2 * pair + row // GROUP, 1.0, 0.0).astype(BF16)

    def group_at(x_of, core_of, g):
        return ((lax.rem(x_of + XS, XS) * CORES + core_of) * ZHI + lax.rem(z_hi + g, ZHI)) * YS

    def prepare(first):
        rows = feats[pl.ds(first, YS)].reshape(YS * SHARE, LANES)
        grads = rows[:, RANK:]
        span = pl.ds(pl.multiple_of(first * SHARE, YS * SHARE), YS * SHARE)
        twice[span, :] = jnp.concatenate([grads, grads], axis=1)
        hid_t[:, span] = dot(select, rows, NT)

    def give(first, to, sends, recvs):
        ref = feats.at[pl.ds(first, YS)]
        send(ref, ref, sends, recvs, to)

    piece = feats.at[pl.ds(0, YS)]
    events = [(0, g) for g in range(ZHI)] + [(s, g) for g in range(ZHI) for s in (1, 3, 2)]

    def from_twin(s, g):
        wait(c_recv.at[s, g], piece)
        prepare(group_at(x + s, 1 - core, g))

    for n, (s, g) in enumerate(events):
        first = group_at(x + s, core, g)
        if s == 0:
            wait(y_recv.at[g], feats.at[pl.ds(0, YS - 1 if g == 0 else YS)])
            give(first, far, x_send.at[2, g], x_recv.at[2, g])
            give(first, left, x_send.at[1, g], x_recv.at[1, g])
            give(first, right, x_send.at[3, g], x_recv.at[3, g])
        else:
            wait(x_recv.at[s, g], piece)
        give(first, twin, c_send.at[s, g], c_recv.at[s, g])
        prepare(first)
        if n >= 2:
            from_twin(*events[n - 2])
    for s, g in events[-2:]:
        from_twin(s, g)
    wait(p_recv, query_in.at[pl.ds(0, ZLO - 1)])

    tokens = [pl.ds(c * SEQ_LEN, SEQ_LEN) for c in range(DPS)]

    def split(values):
        high = values.astype(BF16).astype(F32)
        return jnp.where(low, high, values - high).astype(BF16)

    def image(values, exact):
        operand = split(values)
        seen = [dot(operand, twice[span, :], NT) for span in tokens]
        sums, scaled = [], []
        for c in range(DPS):
            hidden = hid_t[:, tokens[c]]
            sums.append(jnp.sum(seen[c] * hidden, axis=0, keepdims=True))
            weighted = hidden * sums[c]
            high = weighted.astype(BF16)
            if exact:
                high = jnp.concatenate([high, (weighted - high.astype(F32)).astype(BF16)], axis=0)
            scaled.append(high)
        acc = dot(jnp.concatenate(scaled, axis=1), twice[...])
        if exact:
            acc = acc[:RANK] + acc[RANK:]
        return acc * (1.0 / (DPS * SEQ_LEN)) + DAMPING * values, jnp.concatenate(sums, axis=0)

    def advance(carried, exact):
        solved, residual, direction, applied, sums, token_sums, norm_last = carried
        norm_now = total(residual * residual)
        applied_res, sums_res = image(residual, exact)
        ratio = norm_now / norm_last
        direction = residual + ratio * direction
        applied = applied_res + ratio * applied
        sums = sums_res + ratio * sums
        step_size = norm_now / total(direction * applied)
        solved = solved + step_size * direction
        token_sums = token_sums + step_size * sums
        return solved, residual, direction, applied, sums, token_sums, norm_now, step_size

    def iterate(exact, _, carried):
        solved, residual, direction, applied, sums, token_sums, norm_now, step_size = advance(carried, exact)
        residual = residual - step_size * applied
        return solved, residual, direction, applied, sums, token_sums, norm_now

    loaded = query_in[...].reshape(GROUP, LANES)
    turned = jnp.concatenate([loaded[:, RANK:], loaded[:, :RANK]], axis=1)
    low_half = low[:GROUP]
    start = jnp.concatenate([jnp.where(low_half, loaded, turned), jnp.where(low_half, turned, loaded)], axis=0)
    none, no_sums = jnp.zeros_like(start), jnp.zeros((DPS, SEQ_LEN), F32)
    carried = (none, start, none, none, no_sums, no_sums, jnp.ones((1, 1), F32))
    carried = lax.fori_loop(0, EXACT, functools.partial(iterate, True), carried)
    carried = lax.fori_loop(EXACT, ITERS - 1, functools.partial(iterate, False), carried)
    solved, _, _, _, _, token_sums, _, _ = advance(carried, False)

    packed = jnp.where(low_half, solved[:GROUP], solved[GROUP:])
    for i in range(GROUP):
        sol_out[i] = packed[i : i + 1, :]
    sol_in[query] = sol_out[z_lo * YS + y]
    for k in (6, 7, 1, 0):
        to_y = lax.rem(y + k, YS)
        for j in range(ZLO):
            if (k, j) != (0, 0):
                to_z = lax.rem(z_lo + j, ZLO)
                send(
                    sol_out.at[to_z * YS + to_y], sol_in.at[query], o_send, o_recv, at(dp, to_y * ZLO + to_z)
                )

    seq_of_row = lax.broadcasted_iota(jnp.int32, (DPS, LANES), 0)
    seq_of_row = lax.rem(seq_of_row, ZHI) * (XS * CORES) + seq_of_row // ZHI
    means = jnp.sum(token_sums, axis=1, keepdims=True) * (1.0 / SEQ_LEN)
    column = lax.broadcasted_iota(jnp.int32, (DPS, LANES), 1)
    score_out[0] = jnp.sum(jnp.where(column == seq_of_row, means, 0.0), axis=0, keepdims=True)

    score_tensor = dp * 2 + score_half
    around = lax.rem(score_tensor // ZLO + YS + 2 - y, YS)
    serves = around < HALF
    self_score = score_tensor == me

    @pl.when(serves)
    def _():
        for to in range(DPS):
            here = jnp.logical_and(to == dp, self_score)

            @pl.when(here)
            def _():
                score_in[score_row] = score_out[0]

            @pl.when(jnp.logical_not(here))
            def _():
                send(score_out.at[0], score_in.at[score_row], s_send, s_recv, at(to, score_tensor))

    wait(o_recv, sol_in.at[pl.ds(0, QUERIES - 1)])
    sol_ref[...] = sol_in[...].reshape(QUERIES, LANES)

    wait(rs_send, arrived)
    wait(z_send, zparts.at[pl.ds(0, ZLO - 1)])
    wait(q_send, query_mid.at[:, :, pl.ds(0, YS - 1)])
    wait(p_send, query_in.at[pl.ds(0, ZLO - 1)])
    wait(y_send, feats.at[pl.ds(0, 2 * YS - 1)])
    for s in range(4):
        for g in range(ZHI):
            if s:
                wait(x_send.at[s, g], piece)
            wait(c_send.at[s, g], piece)
    wait(o_send, sol_in.at[pl.ds(0, QUERIES - 1)])

    rows_in = score_in.at[pl.ds(0, 7)]

    @pl.when(self_score)
    def _():
        wait(s_recv, rows_in)
        wait(s_send, sol_in.at[pl.ds(0, DPS - 1)])

    @pl.when(jnp.logical_not(self_score))
    def _():
        wait(s_recv, score_in)

    @pl.when(jnp.logical_and(serves, jnp.logical_not(self_score)))
    def _():
        wait(s_send, sol_in.at[pl.ds(0, DPS)])

    picked = jnp.where(lax.broadcasted_iota(jnp.int32, (8, LANES), 1) == dp, score_in[...].reshape(8, LANES), 0.0)
    found = jnp.sum(picked, axis=1, keepdims=True)
    diagonal = lax.broadcasted_iota(jnp.int32, (8, 8), 0) == lax.broadcasted_iota(jnp.int32, (8, 8), 1)
    score_ref[...] = jnp.sum(jnp.where(diagonal, found, 0.0), axis=0, keepdims=True)


def finish(sol_ref, score_ref, sol_out_ref, score_out_ref):
    sol_out_ref[...] = sol_ref[...]
    score_out_ref[...] = score_ref[...]


def shards(hidden_rows, out_grads, proj_in, proj_out, queries):
    proj_in, proj_out, queries = proj_in.T, proj_out.T, queries.T
    vmem = pltpu.VMEM
    dma = pltpu.SemaphoreType.DMA
    tokens = DPS * SEQ_LEN
    solved, scores = pl.pallas_call(
        kernel,
        name="influence",
        out_shape=(
            jax.ShapeDtypeStruct((QUERIES, LANES), F32),
            jax.ShapeDtypeStruct((1, 8), F32),
        ),
        in_specs=[pl.BlockSpec(memory_space=pltpu.HBM)] * 5,
        out_specs=(pl.BlockSpec(memory_space=pltpu.VMEM),) * 2,
        scratch_shapes=[
            vmem(hidden_rows.shape, BF16),
            vmem(out_grads.shape, BF16),
            vmem(proj_in.shape, BF16),
            vmem(proj_out.shape, BF16),
            vmem(queries.shape, F32),
            vmem((YS, SHARE, LANES), F32),
            vmem((YS - 1, SHARE, LANES), F32),
            vmem((ZLO, SHARE, LANES), F32),
            vmem((XS * CORES * ZHI * YS, SHARE, LANES), BF16),
            vmem((2, HALF, 2, 1, LANES), F32),
            vmem((2, 2, YS, 1, LANES), F32),
            vmem((ZLO, YS, 1, LANES), F32),
            vmem((GROUP, 1, LANES), F32),
            vmem((QUERIES, 1, LANES), F32),
            vmem((1, 1, LANES), F32),
            vmem((8, 1, LANES), F32),
            vmem((tokens, LANES), BF16),
            vmem((RANK, tokens), F32),
            dma((5,)),
            pltpu.SemaphoreType.REGULAR,
            dma, dma, dma, dma, dma, dma, dma, dma,
            dma, dma((2,)), dma((4, 2)), dma((4, 2)), dma((4, 2)), dma((4, 2)),
            dma, dma, dma, dma,
        ],
        compiler_params=pltpu.CompilerParams(
            collective_id=0, has_side_effects=True, vmem_limit_bytes=63 << 20
        ),
    )(hidden_rows, out_grads, proj_in, proj_out, queries)
    solved, scores = pl.pallas_call(
        finish,
        name="finish",
        out_shape=(jax.ShapeDtypeStruct(solved.shape, F32), jax.ShapeDtypeStruct(scores.shape, F32)),
    )(solved, scores)
    return solved.T, scores.T


def solution(mesh):
    return jax.shard_map(
        shards,
        mesh=mesh,
        in_specs=(
            P("dp", "tensor"),
            P("dp", "tensor"),
            P("tensor", None),
            P("tensor", None),
            P("tensor", "dp"),
        ),
        out_specs=(P("tensor", "dp"), P("tensor", "dp")),
        check_vma=False,
    )
```

time: 2150 us -> 50.6 us (0.02)
  blocking collectives: 1940 us -> 0 us
  waiting for transfers between devices: 154 us -> 0 us
  Pallas kernels: 0 us -> 49.8 us
    psum x16 -> x0, blocking collectives: 1050 us -> none  [the longest x8 492 us: squares(): return lax.psum(jnp.sum(vectors * vectors, axis=0), 'tensor')]
    all_gather x9 -> x0, blocking collectives: 825 us -> none  [the longest x8 491 us: shards(): lax.all_gather(direction, 'tensor', axis=0, tiled=True)]
    psum x1 -> x0, waiting for transfers between devices: 154 us -> none  [shards(): fisher_sum = lax.psum(local_sum, 'dp')]
    unnamed x1 -> x0, blocking collectives: 62.1 us -> none
    pallas_call x0 -> x2, Pallas kernels: none -> 49.8 us  [the longest x1 48.5 us: shards(): pl.pallas_call(kernel, name='influence', out_shape=(jax.ShapeDtypeStruct(...]
  transfers between devices with their start and end apart: 1 -> 0, of which waited for: 1 -> 0; matrix products, arithmetic and copies ran while one was open for 0% -> 0% of each run, Pallas kernels for 0% -> 0%
where the time goes in v1:
time: 50.6 us; the launch traced here: 50.4 us
  Pallas kernels  49.8 us (98%)
  between operations  0.64 us (1%)
    pallas_call x1, Pallas kernels, shards(): pl.pallas_call(kernel, name='influence', out_shape=(jax.ShapeDtypeStruct(...  48.5 us
    pallas_call x1, Pallas kernels, shards(): pl.pallas_call(finish, name='finish', out_shape=(jax.ShapeDtypeStruct(sol...  1.3 us

profile of v1, /device:TPU:1, one launch (start us, length us, event | category | flops | bytes accessed | tf_op | source)
XLA Modules:
  0.0 50.4 jit_solution(16232784840749331492)
XLA Ops:
  0.6 48.5 %influence.1 = (f32[16,128]{1,0:T(8,128)}, f32[1,8]{1,0:T(1,128)}) custom-call(bf16[256,896]{1,0:T(8,128)(2,1)} %hid_hbm.1, bf16[256,256]{1,0:T(8,128)(2,1)} %grad_hbm.1, bf16[64,896]{1,0:T(8,128)(2,1)} %bitcast.5, bf16[64,256]{1,0:T(8,128)(2,1)} %bitcast.6, f32[16,128]{1,0:T(8,128)} %bitcast.7), custom_call_target="tpu_custom_call" | custom-call | tf_op jit(solution)/shard_map/influence/pallas_call | solution.py:332
  49.1 1.3 %finish.1 = (f32[16,128]{1,0:T(8,128)}, f32[1,8]{1,0:T(1,128)}) custom-call(f32[16,128]{1,0:T(8,128)} %get-tuple-element.6.sol_ref, f32[1,8]{1,0:T(1,128)} %get-tuple-element.7.score_ref), custom_call_target="tpu_custom_call" | custom-call | tf_op jit(solution)/shard_map/finish/pallas_call | solution.py:370

commit v2 on v1

--- a/solution.py
+++ b/solution.py
@@ -42,7 +42,7 @@
     hid_v, grad_v, pin_v, pout_v, query_v,
     part, arrived, zparts, feats,
     query_out, query_mid, query_in, sol_out, sol_in, score_out, score_in,
-    twice, hid_t,
+    twice, hid_t, grad_t,
     load_sem, ready_sem, rs_send, rs_recv, z_send, z_recv, q_send, q_recv, p_send, p_recv,
     y_send, y_recv, x_send, x_recv, c_send, c_recv, o_send, o_recv, s_send, s_recv,
 ):
@@ -156,6 +156,8 @@
     low = lane < RANK
     pair = lax.rem(row, YS) * ZLO + lax.rem(row, GROUP) // YS
     select = jnp.where(lane == 2 * pair + row // GROUP, 1.0, 0.0).astype(BF16)
+    select_grads = jnp.where(lane == RANK + row, 1.0, 0.0).astype(BF16)
+    select_grads = jnp.concatenate([select_grads, select_grads], axis=0)
 
     def group_at(x_of, core_of, g):
         return ((lax.rem(x_of + XS, XS) * CORES + core_of) * ZHI + lax.rem(z_hi + g, ZHI)) * YS
@@ -166,6 +168,7 @@
         span = pl.ds(pl.multiple_of(first * SHARE, YS * SHARE), YS * SHARE)
         twice[span, :] = jnp.concatenate([grads, grads], axis=1)
         hid_t[:, span] = dot(select, rows, NT)
+        grad_t[:, span] = dot(select_grads, rows, NT).astype(BF16)
 
     def give(first, to, sends, recvs):
         ref = feats.at[pl.ds(first, YS)]
@@ -203,7 +206,7 @@
 
     def image(values, exact):
         operand = split(values)
-        seen = [dot(operand, twice[span, :], NT) for span in tokens]
+        seen = [dot(operand, grad_t[:, span]) for span in tokens]
         sums, scaled = [], []
         for c in range(DPS):
             hidden = hid_t[:, tokens[c]]
@@ -357,6 +360,7 @@
             vmem((8, 1, LANES), F32),
             vmem((tokens, LANES), BF16),
             vmem((RANK, tokens), F32),
+            vmem((LANES, tokens), BF16),
             dma((5,)),
             pltpu.SemaphoreType.REGULAR,
             dma, dma, dma, dma, dma, dma, dma, dma,

time: 50.6 us -> 49.3 us (0.974)
  Pallas kernels: 49.8 us -> 48.5 us
    pallas_call x1, Pallas kernels: 48.5 us -> 47.2 us  [shards(): pl.pallas_call(kernel, name='influence', out_shape=(jax.ShapeDtypeStruct(...]
where the time goes in v2:
time: 49.3 us; the launch traced here: 49.2 us
  Pallas kernels  48.5 us (98%)
  between operations  0.64 us (1%)
    pallas_call x1, Pallas kernels, shards(): pl.pallas_call(kernel, name='influence', out_shape=(jax.ShapeDtypeStruct(...  47.2 us
    pallas_call x1, Pallas kernels, shards(): pl.pallas_call(finish, name='finish', out_shape=(jax.ShapeDtypeStruct(sol...  1.3 us

profile of v2, /device:TPU:1, one launch (start us, length us, event | category | flops | bytes accessed | tf_op | source)
XLA Modules:
  0.0 49.2 jit_solution(14369445643721844463)
XLA Ops:
  0.6 47.2 %influence.1 = (f32[16,128]{1,0:T(8,128)}, f32[1,8]{1,0:T(1,128)}) custom-call(bf16[256,896]{1,0:T(8,128)(2,1)} %hid_hbm.1, bf16[256,256]{1,0:T(8,128)(2,1)} %grad_hbm.1, bf16[64,896]{1,0:T(8,128)(2,1)} %bitcast.5, bf16[64,256]{1,0:T(8,128)(2,1)} %bitcast.6, f32[16,128]{1,0:T(8,128)} %bitcast.7), custom_call_target="tpu_custom_call" | custom-call | tf_op jit(solution)/shard_map/influence/pallas_call | solution.py:335
  47.9 1.3 %finish.1 = (f32[16,128]{1,0:T(8,128)}, f32[1,8]{1,0:T(1,128)}) custom-call(f32[16,128]{1,0:T(8,128)} %get-tuple-element.6.sol_ref, f32[1,8]{1,0:T(1,128)} %get-tuple-element.7.score_ref), custom_call_target="tpu_custom_call" | custom-call | tf_op jit(solution)/shard_map/finish/pallas_call | solution.py:374
